TPU v7x, 32 devices: a whole 2x2x4 slice. The times are simulated.
32 devices in a mesh: parts: 2 (over x), train: 8 (over z, y), layer: 2 (over core).
Axes of the slice: x: 2, y: 2, z: 4, core: 2. Of those that a mesh axis runs over, the one named last changes fastest.
Arguments:
- train_inputs: bfloat16 [2, 32, 192, 4096], P('layer', ('parts', 'train')), parts along dimension 1, may hold values from -6 to 6
- train_grads: bfloat16 [2, 32, 192, 4096], P('layer', ('parts', 'train')), parts along dimension 1, may hold values from -6 to 6
- query_inputs: bfloat16 [2, 128, 32, 4096], P('layer', ('parts', 'train')), parts along dimension 1, may hold values from -6 to 6
- query_grads: bfloat16 [2, 128, 32, 4096], P('layer', ('parts', 'train')), parts along dimension 1, may hold values from -6 to 6
- in_project: bfloat16 [2, 4096, 64], P('layer'), may hold values from -0.09375 to 0.09375
- out_project: bfloat16 [2, 4096, 64], P('layer'), may hold values from -0.09375 to 0.09375
- in_factor: float32 [2, 64, 64], P('layer'), as said below
- out_factor: float32 [2, 64, 64], P('layer'), as said below
- train_lengths: int32 [32], P(('parts', 'train')), parts along dimension 0, may hold values from 1 to 192, as said below
- query_lengths: int32 [128], P(('parts', 'train')), parts along dimension 0, may hold values from 1 to 32, as said below
Outputs:
- scores: float32 [32, 64], P(('parts', 'train'), 'layer'), parts along dimension 0
There are 2 independent parts, one for each index of `parts`. A program takes and returns all parts, laid end to end along the dimension named above; an argument that names none is the same for every part. Nothing has to cross between parts.
Inputs may be any that keep to these rules, and one draw needn't show every extreme that they name: `train_lengths`: at least one training sequence has exactly 192 tokens. `query_lengths`: at least one query sequence has exactly 32 tokens. `in_factor`: Symmetric, with each diagonal entry larger than the sum of magnitudes of its row's other entries. `out_factor`: Symmetric, with each diagonal entry larger than the sum of magnitudes of its row's other entries.
All inputs are finite; a program needn't handle non-finite values.
Results may differ from a plain program's by a relative error of at most 0.0043.
Values may be sent and summed in bfloat16 or wider, within the bound.
A program may use at most 64 MiB of HBM per device.

v0:
```python
import jax
import jax.numpy as jnp
from jax import lax
from jax.sharding import PartitionSpec as P


def project(inputs, grads, lengths, in_weight, out_weight):
    xp = jnp.einsum("std,dr->str", inputs, in_weight, preferred_element_type=jnp.float32)
    gp = jnp.einsum("std,dr->str", grads, out_weight, preferred_element_type=jnp.float32)
    steps = lax.broadcasted_iota(jnp.int32, gp.shape[:2], 1)
    mask = (steps < lengths[:, None]).astype(jnp.float32)
    gp = gp * mask[:, :, None]
    outer = jnp.einsum("sto,sti->soi", gp, xp, precision=lax.Precision.HIGHEST)
    return outer / lengths[:, None, None].astype(jnp.float32)


def on_device(
    train_inputs,
    train_grads,
    query_inputs,
    query_grads,
    in_project,
    out_project,
    in_factor,
    out_factor,
    train_lengths,
    query_lengths,
):
    train_count = train_inputs.shape[1]
    query_count = query_inputs.shape[1]
    train_grad = project(
        train_inputs[0], train_grads[0], train_lengths, in_project[0], out_project[0]
    )
    train_rows = [train_grad.reshape(train_count, -1).astype(jnp.bfloat16)]
    query_grad = project(
        query_inputs[0], query_grads[0], query_lengths, in_project[0], out_project[0]
    )
    conditioned = jnp.einsum(
        "ab,sbc,cd->sad", out_factor[0], query_grad, in_factor[0], precision=lax.Precision.HIGHEST
    )
    query_rows = [conditioned.reshape(query_count, -1).astype(jnp.bfloat16)]
    train_block = jnp.stack(train_rows)
    query_block = jnp.stack(query_rows)
    partial_scores = jnp.einsum(
        "lsk,lqk->sq",
        train_block,
        lax.all_gather(query_block, "train", axis=1, tiled=True),
        preferred_element_type=jnp.float32,
    )
    return lax.psum_scatter(partial_scores, "layer", scatter_dimension=1, tiled=True)


def solution(mesh):
    in_specs = (
        P("layer", ("parts", "train"), None, None),
        P("layer", ("parts", "train"), None, None),
        P("layer", ("parts", "train"), None, None),
        P("layer", ("parts", "train"), None, None),
        P("layer", None, None),
        P("layer", None, None),
        P("layer", None, None),
        P("layer", None, None),
        P(("parts", "train")),
        P(("parts", "train")),
    )
    out_specs = P(("parts", "train"), "layer")
    return jax.shard_map(
        on_device, mesh=mesh, in_specs=in_specs, out_specs=out_specs, check_vma=False
    )
```

profile of v0, /device:TPU:1, one launch (start us, length us, event | category | flops | bytes accessed | tf_op | source)
XLA Modules:
  0.0 70.5 jit_solution(9859594383702782127)
XLA Ops:
  6.5 0.0 copy-start
  6.5 0.0 reduce-scatter.4.cloned.1.call-start
  6.5 0.0 copy-start.1
  6.5 0.0 copy-start.2
  6.5 0.8 %convert_element_type.44 = f32[2]{0:T(128)S(1)} convert(s32[2]{0:T(128)} %param.18) | non-fusion elementwise | flops 2 | bytes 16 | tf_op jit(solution)/shard_map/convert_element_type | solution.py:14
  7.4 1.1 %compare_convert_fusion = f32[2,192]{1,0:T(2,128)S(1)} fusion(s32[2]{0:T(128)} %param.18), kind=kLoop, calls=%fused_computation.25 | loop fusion | flops 768 | bytes 1544 | tf_op jit(solution)/shard_map/convert_element_type | solution.py:11
  8.5 0.7 %convert_element_type.48 = f32[8]{0:T(128)S(1)} convert(s32[8]{0:T(128)} %param.19) | non-fusion elementwise | flops 8 | bytes 64 | tf_op jit(solution)/shard_map/convert_element_type | solution.py:14
  9.2 0.7 %fusion.23 = f32[8,32]{1,0:T(8,128)S(1)} fusion(s32[8]{0:T(128)} %param.19), kind=kLoop, calls=%fused_computation.24 | loop fusion | flops 512 | bytes 1056 | tf_op jit(solution)/shard_map/convert_element_type | solution.py:11
  10.0 0.0 copy-done
  10.0 2.1 %fusion = f32[2,192,64]{1,2,0:T(8,128)S(1)} fusion(bf16[1,2,192,4096]{3,2,1,0:T(8,128)(2,1)S(1)} %copy-done, bf16[1,4096,64]{1,2,0:T(8,128)(2,1)} %param.14), kind=kOutput, calls=%fused_computation | convolution fusion | flops 201326592 | bytes 3768320 | tf_op jit(solution)/shard_map/std,dr->str/dot_general | solution.py:8
  12.1 0.0 copy-done.1
  12.1 0.0 copy-done.2
  12.1 1.1 %fusion.11 = f32[2,192,64]{1,2,0:T(8,128)S(1)} fusion(bf16[1,2,192,4096]{3,2,1,0:T(8,128)(2,1)S(1)} %copy-done.1, bf16[1,4096,64]{1,2,0:T(8,128)(2,1)S(1)} %copy-done.2, f32[2,192]{1,0:T(2,128)S(1)} %compare_convert_fusion), kind=kOutput, calls=%fused_computation.11 | convolution fusion | flops 201351168 | bytes 3769856 | tf_op jit(solution)/shard_map/std,dr->str/dot_general | solution.py:9
  13.2 0.3 fusion.14
  13.5 0.1 convert_element_type.46
  13.6 0.0 copy-start.3
  13.6 0.0 copy-start.4
  13.6 2.4 %fusion.4 = f32[8,32,64]{2,1,0:T(8,128)S(1)} fusion(bf16[1,8,32,4096]{3,2,1,0:T(8,128)(2,1)} %param.12, bf16[1,4096,64]{1,2,0:T(8,128)(2,1)} %param.14), kind=kOutput, calls=%fused_computation.4 | convolution fusion | flops 134217728 | bytes 2686976 | tf_op jit(solution)/shard_map/std,dr->str/dot_general | solution.py:8
  16.0 2.4 %fusion.8 = f32[8,32,64]{2,1,0:T(8,128)S(1)} fusion(bf16[1,8,32,4096]{3,2,1,0:T(8,128)(2,1)} %param.13, bf16[1,4096,64]{1,2,0:T(8,128)(2,1)} %param.15, f32[8,32]{1,0:T(8,128)S(1)} %fusion.23), kind=kOutput, calls=%fused_computation.10 | convolution fusion | flops 134234112 | bytes 2688000 | tf_op jit(solution)/shard_map/std,dr->str/dot_general | solution.py:9
  18.4 0.6 convolution_divide_fusion
  19.0 0.0 copy-done.3
  19.0 0.4 fusion.21
  19.4 0.0 copy-done.4
  19.4 0.4 convolution_convert_fusion
  19.8 0.2 convert_element_type.50
  20.0 26.9 %all_gather.3 = bf16[1,64,4096]{2,1,0:T(8,128)(2,1)S(1)} all-gather(bf16[1,8,4096]{2,1,0:T(8,128)(2,1)S(1)} %convert_element_type.50), channel_id=1, replica_groups=mesh['parts'=2,'train'=8,'layer'=2] {'train'}, dimensions={1}, use_global_device_ids=true | all-gather | bytes 589824 | tf_op jit(solution)/shard_map/all_gather | solution.py:47
  46.9 0.9 %convolution_bitcast_fusion = f32[64,2]{1,0:T(8,128)} fusion(bf16[2,4096]{1,0:T(2,128)(2,1)S(1)} %convert_element_type.46, bf16[1,64,4096]{2,1,0:T(8,128)(2,1)S(1)} %all_gather.3), kind=kOutput, calls=%fused_computation.14 | convolution fusion | flops 1048576 | bytes 541184
  47.8 0.0 reduce-scatter.4.cloned.1.call-update
  47.8 14.5 %reduce-scatter.4.cloned.1.call-done = f32[32,2]{1,0:T(8,128)} async-done(((f32[64,2]{1,0:T(8,128)}), f32[32,2]{1,0:T(8,128)}) %reduce-scatter.4.cloned.1.call-update) | async-done | bytes 272
  62.3 1.4 %copy.12 = f32[2,32]{1,0:T(2,128)} copy(f32[2,32]{0,1:T(8,128)} %bitcast.49) | data formatting | bytes 512
Async XLA Ops:
  6.5 3.4 %copy-start = (bf16[1,2,192,4096]{3,2,1,0:T(8,128)(2,1)S(1)}, bf16[1,2,192,4096]{3,2,1,0:T(8,128)(2,1)}, u32[]{:S(2)}) copy-start(bf16[1,2,192,4096]{3,2,1,0:T(8,128)(2,1)} %param.10) | copy-start | bytes 9437188
  6.5 55.8 %reduce-scatter.4.cloned.1.call-start = ((), (), s32[]{:S(2)}) async-start(), calls=%async_computation.1 | async-start | bytes 49152
  6.5 5.6 %copy-start.1 = (bf16[1,2,192,4096]{3,2,1,0:T(8,128)(2,1)S(1)}, bf16[1,2,192,4096]{3,2,1,0:T(8,128)(2,1)}, u32[]{:S(2)}) copy-start(bf16[1,2,192,4096]{3,2,1,0:T(8,128)(2,1)} %param.11) | copy-start | bytes 9437188
  6.5 5.6 %copy-start.2 = (bf16[1,4096,64]{1,2,0:T(8,128)(2,1)S(1)}, bf16[1,4096,64]{1,2,0:T(8,128)(2,1)}, u32[]{:S(2)}) copy-start(bf16[1,4096,64]{1,2,0:T(8,128)(2,1)} %param.15) | copy-start | bytes 1572868
  13.6 5.4 %copy-start.3 = (f32[1,64,64]{2,1,0:T(8,128)S(1)}, f32[1,64,64]{2,1,0:T(8,128)}, u32[]{:S(2)}) copy-start(f32[1,64,64]{2,1,0:T(8,128)} %param.17) | copy-start | bytes 49156
  13.6 5.8 %copy-start.4 = (f32[1,64,64]{2,1,0:T(8,128)S(1)}, f32[1,64,64]{2,1,0:T(8,128)}, u32[]{:S(2)}) copy-start(f32[1,64,64]{2,1,0:T(8,128)} %param.16) | copy-start | bytes 49156
Sparse Core Ops, SparseCore 0:
  47.9 14.3 reduce-scatter.3
where the time goes:
time: 71.1 us; the launch traced here: 70.5 us
  blocking collectives  26.9 us (38%)
  waiting for transfers between devices  14.5 us (20%)
  between operations  13.5 us (19%)
  matrix products  10.5 us (15%)
  other arithmetic  3.4 us (5%)
  local copies, waits for them, and re-layouts  1.65 us (2%)
    all_gather x1, blocking collectives, on_device(): lax.all_gather(query_block, 'train', axis=1, tiled=True)  26.9 us
    unnamed x2, waiting for transfers between devices  14.5 us
    dot_general x2, matrix products, project(): jnp.einsum('std,dr->str', inputs, in_weight, preferred_element_type=jnp.f...  4.52 us
    dot_general x2, matrix products, project(): jnp.einsum('std,dr->str', grads, out_weight, preferred_element_type=jnp.f...  3.48 us
    convert_element_type x2, other arithmetic, project(): mask = (steps < lengths[:, None]).astype(jnp.float32)  1.85 us
    convert_element_type x2, other arithmetic, project(): return outer / lengths[:, None, None].astype(jnp.float32)  1.55 us
  transfers between devices with their start and end apart: 1, of which 1 were waited for; matrix products, arithmetic and copies ran while one was open for 0% of the time, Pallas kernels for 0%

commit v1 on v0

v1 whole, which is shorter than its diff:
```python
import functools

import jax
import jax.numpy as jnp
from jax import lax
from jax.experimental import pallas as pl
from jax.experimental.pallas import tpu as pltpu
from jax.sharding import PartitionSpec as P

MESH = pl.DeviceIdType.MESH
F32 = jnp.float32
BF16 = jnp.bfloat16
SPLITS = 4


def dot_nt(a, b):
    return lax.dot_general(a, b, (((1,), (1,)), ((), ())), preferred_element_type=F32)


def dot_nn(a, b):
    return lax.dot_general(a, b, (((1,), (0,)), ((), ())), preferred_element_type=F32)


def halves(a):
    high = a.astype(BF16)
    return high, (a - high.astype(F32)).astype(BF16)


def fine(dot, a, b):
    return dot(a[0], b[0]) + (dot(a[0], b[1]) + dot(a[1], b[0]))


def lanes(shape):
    return lax.broadcasted_iota(jnp.int32, shape, len(shape) - 1)


def repeat(count, body):
    if count <= 8:
        for step in range(count):
            body(step)
    else:
        lax.fori_loop(0, count, lambda step, carry: (body(step), carry)[1], 0)


def kernel(
    n,
    xt, gt, xq, gq, win, wout, fin, fout, lt, lq,
    out,
    xt_v, gt_v, xq_v, gq_v, win_v, wout_v, fin_v, fout_v, lt_s, lq_s,
    held, wide, query, mine, landed,
    in_sem, far_sem, small_sem, send_one, recv_one, send_two, recv_two,
):
    trains, slots, width = xt.shape
    queries = lq.shape[0]
    short = xq.shape[0] // queries
    rank = win.shape[0]
    tokens = queries * short
    part = width // SPLITS
    me, layer = lax.axis_index("train"), lax.axis_index("layer")
    half = n // 2
    owner = me // half
    place = lax.rem(me, half)

    small = [
        pltpu.make_async_copy(src, dst, small_sem.at[k])
        for k, (src, dst) in enumerate(((lt, lt_s), (lq, lq_s), (fin, fin_v), (fout, fout_v)))
    ]
    load_win = pltpu.make_async_copy(win, win_v, in_sem.at[0])
    load_wout = pltpu.make_async_copy(wout, wout_v, in_sem.at[1])
    load_x = [pltpu.make_async_copy(xt.at[s], xt_v.at[s], in_sem.at[2 + 2 * s]) for s in range(trains)]
    load_g = [pltpu.make_async_copy(gt.at[s], gt_v.at[s], in_sem.at[3 + 2 * s]) for s in range(trains)]
    cut = [pl.ds(k * part, part) for k in range(SPLITS)]
    load_gq = [pltpu.make_async_copy(gq.at[:, c], gq_v.at[:, c], far_sem.at[k]) for k, c in enumerate(cut)]
    load_xq = [pltpu.make_async_copy(xq.at[:, c], xq_v.at[:, c], far_sem.at[SPLITS + k]) for k, c in enumerate(cut)]
    load_win.start()
    load_x[0].start()
    load_wout.start()
    load_g[0].start()
    for copy in small:
        copy.start()
    for s in range(1, trains):
        load_x[s].start()
        load_g[s].start()
    for copy in load_gq + load_xq:
        copy.start()

    barrier = pltpu.get_barrier_semaphore()

    def greet(step):
        for other in range(2):
            @pl.when(jnp.logical_or(step != me, other != layer))
            def _():
                pl.semaphore_signal(
                    barrier, inc=1, device_id={"train": step, "layer": other}, device_id_type=MESH
                )

    repeat(n, greet)

    for s in range(trains):
        if s == 0:
            load_win.wait()
        load_x[s].wait()
        xp = dot_nt(win_v[...], xt_v[s])
        if s == 0:
            load_wout.wait()
        load_g[s].wait()
        gp = dot_nt(wout_v[...], gt_v[s])
        if s == 0:
            for copy in small:
                copy.wait()
        length = jnp.full((1, slots), lt_s[s], jnp.int32)
        scale = jnp.where(lanes((1, slots)) < length, 1.0 / length.astype(F32), 0.0)
        both = fine(dot_nt, halves(gp * scale), halves(jnp.concatenate([xp, xp], axis=0)))
        packed = jnp.where(lanes((rank // 2, 2 * rank)) < rank, both[: rank // 2], both[rank // 2 :])
        held[me, s] = packed.astype(BF16)

    pl.semaphore_wait(barrier, 2 * n - 1)

    def first(slot, peer, k):
        return pltpu.make_async_remote_copy(
            src_ref=held.at[slot],
            dst_ref=held.at[slot],
            send_sem=send_one.at[k],
            recv_sem=recv_one.at[slot],
            device_id={"train": peer},
            device_id_type=MESH,
        )

    def send_first(k):
        first(me, lax.rem(me + 1 + k, n), k).start()

    repeat(n - 1, send_first)

    token = lanes((1, tokens))
    length = jnp.full((1, tokens), lq_s[0], jnp.int32)
    for j in range(1, queries):
        length = jnp.where(token // short == j, lq_s[j], length)
    scale = jnp.where(lax.rem(token, short) < length, 1.0 / length.astype(F32), 0.0)
    gp = jnp.zeros((rank, tokens), F32)
    for k, c in enumerate(cut):
        load_gq[k].wait()
        gp += dot_nt(wout_v[:, c], gq_v[:, c])
    gp = fine(dot_nn, halves(fout_v[...]), halves(gp * scale))
    block = (
        lanes((1, queries, tokens)) // short == lax.broadcasted_iota(jnp.int32, (1, queries, tokens), 1)
    ).astype(F32)
    spread = halves((gp[:, None, :] * block).reshape(rank * queries, tokens))
    xp = jnp.zeros((rank, tokens), F32)
    for k, c in enumerate(cut):
        load_xq[k].wait()
        xp += dot_nt(win_v[:, c], xq_v[:, c])
    xp = fine(dot_nn, halves(fin_v[...]), halves(xp))
    both = fine(dot_nt, spread, halves(jnp.concatenate([xp, xp], axis=0)))
    rows = rank // 2 * queries
    query[...] = (
        jnp.where(lanes((rows, 2 * rank)) < rank, both[:rows], both[rows:]).astype(BF16).astype(F32)
    )

    def second(peer, to, where, source, k):
        return pltpu.make_async_remote_copy(
            src_ref=mine.at[k],
            dst_ref=landed.at[where, source],
            send_sem=send_two.at[k],
            recv_sem=recv_two.at[where, source],
            device_id={"train": peer, "layer": to},
            device_id_type=MESH,
        )

    def own(k):
        return pltpu.make_async_copy(mine.at[k], landed.at[place, layer], recv_two.at[place, layer])

    def score(k):
        peer = lax.rem(me + 1 + k, n)
        if isinstance(k, int):
            if k < n - 1:
                first(peer, peer, k).wait_recv()
        else:
            @pl.when(k < n - 1)
            def _():
                first(peer, peer, k).wait_recv()
        sums = []
        for s in range(trains):
            wide[...] = held[peer, s].astype(F32)
            total = jnp.zeros((queries, 2 * rank), F32)
            for a in range(rank // 2):
                total += wide[a : a + 1, :] * query[a * queries : (a + 1) * queries, :]
            sums.append(total + pltpu.roll(total, rank, 1))
        mine[k] = jnp.where(lanes((queries, 2 * rank)) < rank, sums[0], sums[1])
        local = jnp.logical_and(peer == me, owner == layer)

        @pl.when(jnp.logical_not(local))
        def _():
            second(peer, owner, place, layer, k).start()

        @pl.when(local)
        def _():
            own(k).start()

    repeat(n, score)

    def collect(where):
        for source in range(2):
            origin = layer * half + where
            local = jnp.logical_and(origin == me, source == layer)

            @pl.when(jnp.logical_not(local))
            def _():
                second(me, layer, where, source, 0).wait_recv()

            @pl.when(local)
            def _():
                own(n - 1).wait()

    repeat(half, collect)
    total = (landed[:, 0] + landed[:, 1]).reshape(half * queries, 2 * rank)
    high, low = halves(total)
    rest = (total - high.astype(F32) - low.astype(F32)).astype(BF16)
    pick = (
        lanes((8, 2 * rank)) // rank == lax.broadcasted_iota(jnp.int32, (8, 2 * rank), 0)
    ).astype(F32).astype(BF16)
    result = dot_nt(pick, high) + (dot_nt(pick, low) + dot_nt(pick, rest))
    out[...] = result[:trains]

    def finish_first(k):
        first(me, lax.rem(me + 1 + k, n), k).wait_send()

    repeat(n - 1, finish_first)

    def finish_second(k):
        peer = lax.rem(me + 1 + k, n)

        @pl.when(jnp.logical_not(jnp.logical_and(peer == me, owner == layer)))
        def _():
            second(peer, owner, place, layer, k).wait_send()

    repeat(n, finish_second)


def on_device(n, xt, gt, xq, gq, win, wout, fin, fout, lt, lq):
    _, trains, slots, width = xt.shape
    _, queries, short, _ = xq.shape
    rank = win.shape[2]
    tokens = queries * short
    half = n // 2
    return pl.pallas_call(
        functools.partial(kernel, n),
        out_shape=jax.ShapeDtypeStruct((trains, half * queries), F32),
        in_specs=[pl.BlockSpec(memory_space=pl.ANY)] * 10,
        out_specs=pl.BlockSpec(memory_space=pltpu.VMEM),
        scratch_shapes=[
            pltpu.VMEM((trains, slots, width), BF16),
            pltpu.VMEM((trains, slots, width), BF16),
            pltpu.VMEM((tokens, width), BF16),
            pltpu.VMEM((tokens, width), BF16),
            pltpu.VMEM((rank, width), BF16),
            pltpu.VMEM((rank, width), BF16),
            pltpu.VMEM((rank, rank), F32),
            pltpu.VMEM((rank, rank), F32),
            pltpu.SMEM((trains,), jnp.int32),
            pltpu.SMEM((queries,), jnp.int32),
            pltpu.VMEM((n, trains, rank // 2, 2 * rank), BF16),
            pltpu.VMEM((rank // 2, 2 * rank), F32),
            pltpu.VMEM((rank // 2 * queries, 2 * rank), F32),
            pltpu.VMEM((n, queries, 2 * rank), F32),
            pltpu.VMEM((half, 2, queries, 2 * rank), F32),
            pltpu.SemaphoreType.DMA((2 + 2 * trains,)),
            pltpu.SemaphoreType.DMA((2 * SPLITS,)),
            pltpu.SemaphoreType.DMA((4,)),
            pltpu.SemaphoreType.DMA((n,)),
            pltpu.SemaphoreType.DMA((n,)),
            pltpu.SemaphoreType.DMA((n,)),
            pltpu.SemaphoreType.DMA((half, 2)),
        ],
        compiler_params=pltpu.CompilerParams(
            collective_id=0, has_side_effects=True, vmem_limit_bytes=48 * 1024 * 1024
        ),
        cost_estimate=pl.CostEstimate(
            flops=4 * (trains * slots + tokens) * width * rank,
            bytes_accessed=4 * (trains * slots + tokens + rank) * width,
            transcendentals=0,
        ),
    )(
        xt[0], gt[0], xq.reshape(tokens, width), gq.reshape(tokens, width),
        win[0].T, wout[0].T, fin[0], fout[0], lt, lq,
    )


def solution(mesh):
    rows = P("layer", ("parts", "train"), None, None)
    shared = P("layer", None, None)
    counts = P(("parts", "train"))
    return jax.shard_map(
        functools.partial(on_device, mesh.shape["train"]),
        mesh=mesh,
        in_specs=(rows,) * 4 + (shared,) * 4 + (counts,) * 2,
        out_specs=P(("parts", "train"), "layer"),
        check_vma=False,
    )
```

time: 71.1 us -> 26.8 us (0.38)
  the two profiles are of different devices: /device:TPU:1 before, /device:TPU:0 now
where the time goes in v1:
time: 26.8 us; the launch traced here: 26.3 us
  Pallas kernels  17.7 us (66%)
  local copies, waits for them, and re-layouts  8.65 us (32%)
    pallas_call x1, Pallas kernels, on_device(): pl.pallas_call(functools.partial(kernel, n), out_shape=jax.ShapeDtypeStru...  17.7 us
    unnamed x17, local copies, waits for them, and re-layouts  8.65 us

profile of v1, /device:TPU:0, one launch (start us, length us, event | category | flops | bytes accessed | tf_op | source)
XLA Modules:
  0.0 26.3 jit_solution(13526263796506873277)
XLA Ops:
  0.0 0.0 copy-start
  0.0 1.6 %copy-done = bf16[1,8,32,4096]{3,2,1,0:T(8,128)(2,1)S(1)} copy-done((bf16[1,8,32,4096]{3,2,1,0:T(8,128)(2,1)S(1)}, bf16[1,8,32,4096]{3,2,1,0:T(8,128)(2,1)}, u32[]{:S(2)}) %copy-start) | copy-done | bytes 2097176
  1.6 0.0 copy-start.1
  1.6 1.6 %copy-done.1 = bf16[1,8,32,4096]{3,2,1,0:T(8,128)(2,1)S(1)} copy-done((bf16[1,8,32,4096]{3,2,1,0:T(8,128)(2,1)S(1)}, bf16[1,8,32,4096]{3,2,1,0:T(8,128)(2,1)}, u32[]{:S(2)}) %copy-start.1) | copy-done | bytes 2097176
  3.2 0.0 copy-start.2
  3.2 1.0 %copy-done.2 = bf16[1,4096,64]{1,2,0:T(8,128)(2,1)S(1)} copy-done((bf16[1,4096,64]{1,2,0:T(8,128)(2,1)S(1)}, bf16[1,4096,64]{1,2,0:T(8,128)(2,1)}, u32[]{:S(2)}) %copy-start.2) | copy-done | bytes 524312
  4.2 0.0 copy-start.3
  4.2 1.0 %copy-done.3 = bf16[1,4096,64]{1,2,0:T(8,128)(2,1)S(1)} copy-done((bf16[1,4096,64]{1,2,0:T(8,128)(2,1)S(1)}, bf16[1,4096,64]{1,2,0:T(8,128)(2,1)}, u32[]{:S(2)}) %copy-start.3) | copy-done | bytes 524312
  5.3 0.0 copy-start.4
  5.3 0.8 %copy-done.4 = f32[1,64,64]{2,1,0:T(8,128)S(1)} copy-done((f32[1,64,64]{2,1,0:T(8,128)S(1)}, f32[1,64,64]{2,1,0:T(8,128)}, u32[]{:S(2)}) %copy-start.4) | copy-done | bytes 16408
  6.0 0.0 copy-start.5
  6.0 0.8 %copy-done.5 = f32[1,64,64]{2,1,0:T(8,128)S(1)} copy-done((f32[1,64,64]{2,1,0:T(8,128)S(1)}, f32[1,64,64]{2,1,0:T(8,128)}, u32[]{:S(2)}) %copy-start.5) | copy-done | bytes 16408
  6.8 0.0 copy-start.6
  6.8 0.7 %copy-done.6 = s32[2]{0:T(128)S(1)} copy-done((s32[2]{0:T(128)S(1)}, s32[2]{0:T(128)}, u32[]{:S(2)}) %copy-start.6) | copy-done | bytes 32
  7.4 0.0 copy-start.7
  7.4 0.7 %copy-done.7 = s32[8]{0:T(128)S(1)} copy-done((s32[8]{0:T(128)S(1)}, s32[8]{0:T(128)}, u32[]{:S(2)}) %copy-start.7) | copy-done | bytes 56
  8.1 17.7 %shard_map.100 = f32[2,32]{1,0:T(2,128)S(1)} custom-call(bf16[2,192,4096]{2,1,0:T(8,128)(2,1)} %bitcast.18, bf16[2,192,4096]{2,1,0:T(8,128)(2,1)} %bitcast.19, bf16[256,4096]{1,0:T(8,128)(2,1)S(1)} %bitcast.12, bf16[256,4096]{1,0:T(8,128)(2,1)S(1)} %bitcast.13, bf16[64,4096]{1,0:T(8,128)(2,1)S(1)} %bitcast.14, bf16[64,4096]{1,0:T(8,128)(2,1)S(1)} %bitcast.15, ...), custom_call_target="tpu_custom_call" | custom-call | flops 671088640 | bytes 11534336 | tf_op jit(solution)/shard_map/pallas_call | solution.py:245
  25.8 0.6 %copy.12 = f32[2,32]{1,0:T(2,128)} copy(f32[2,32]{1,0:T(2,128)S(1)} %shard_map.100) | data formatting | bytes 512
Async XLA Ops:
  0.0 1.6 %copy-start = (bf16[1,8,32,4096]{3,2,1,0:T(8,128)(2,1)S(1)}, bf16[1,8,32,4096]{3,2,1,0:T(8,128)(2,1)}, u32[]{:S(2)}) copy-start(bf16[1,8,32,4096]{3,2,1,0:T(8,128)(2,1)} %param.12) | copy-start | bytes 6291460
  1.6 1.6 %copy-start.1 = (bf16[1,8,32,4096]{3,2,1,0:T(8,128)(2,1)S(1)}, bf16[1,8,32,4096]{3,2,1,0:T(8,128)(2,1)}, u32[]{:S(2)}) copy-start(bf16[1,8,32,4096]{3,2,1,0:T(8,128)(2,1)} %param.13) | copy-start | bytes 6291460
  3.2 1.0 %copy-start.2 = (bf16[1,4096,64]{1,2,0:T(8,128)(2,1)S(1)}, bf16[1,4096,64]{1,2,0:T(8,128)(2,1)}, u32[]{:S(2)}) copy-start(bf16[1,4096,64]{1,2,0:T(8,128)(2,1)} %param.14) | copy-start | bytes 1572868
  4.2 1.0 %copy-start.3 = (bf16[1,4096,64]{1,2,0:T(8,128)(2,1)S(1)}, bf16[1,4096,64]{1,2,0:T(8,128)(2,1)}, u32[]{:S(2)}) copy-start(bf16[1,4096,64]{1,2,0:T(8,128)(2,1)} %param.15) | copy-start | bytes 1572868
  5.3 0.8 %copy-start.4 = (f32[1,64,64]{2,1,0:T(8,128)S(1)}, f32[1,64,64]{2,1,0:T(8,128)}, u32[]{:S(2)}) copy-start(f32[1,64,64]{2,1,0:T(8,128)} %param.16) | copy-start | bytes 49156
  6.0 0.8 %copy-start.5 = (f32[1,64,64]{2,1,0:T(8,128)S(1)}, f32[1,64,64]{2,1,0:T(8,128)}, u32[]{:S(2)}) copy-start(f32[1,64,64]{2,1,0:T(8,128)} %param.17) | copy-start | bytes 49156
  6.8 0.7 %copy-start.6 = (s32[2]{0:T(128)S(1)}, s32[2]{0:T(128)}, u32[]{:S(2)}) copy-start(s32[2]{0:T(128)} %lt.1) | copy-start | bytes 28
  7.4 0.7 %copy-start.7 = (s32[8]{0:T(128)S(1)}, s32[8]{0:T(128)}, u32[]{:S(2)}) copy-start(s32[8]{0:T(128)} %lq.1) | copy-start | bytes 100

commit v2 on v1

--- a/solution.py
+++ b/solution.py
@@ -34,6 +34,10 @@
     return lax.broadcasted_iota(jnp.int32, shape, len(shape) - 1)
 
 
+def rows_of(shape):
+    return lax.broadcasted_iota(jnp.int32, shape, 0)
+
+
 def repeat(count, body):
     if count <= 8:
         for step in range(count):
@@ -47,7 +51,7 @@
     xt, gt, xq, gq, win, wout, fin, fout, lt, lq,
     out,
     xt_v, gt_v, xq_v, gq_v, win_v, wout_v, fin_v, fout_v, lt_s, lq_s,
-    held, wide, query, mine, landed,
+    held, wide, wide_query, query, mine, landed,
     in_sem, far_sem, small_sem, send_one, recv_one, send_two, recv_two,
 ):
     trains, slots, width = xt.shape
@@ -72,16 +76,7 @@
     cut = [pl.ds(k * part, part) for k in range(SPLITS)]
     load_gq = [pltpu.make_async_copy(gq.at[:, c], gq_v.at[:, c], far_sem.at[k]) for k, c in enumerate(cut)]
     load_xq = [pltpu.make_async_copy(xq.at[:, c], xq_v.at[:, c], far_sem.at[SPLITS + k]) for k, c in enumerate(cut)]
-    load_win.start()
-    load_x[0].start()
-    load_wout.start()
-    load_g[0].start()
-    for copy in small:
-        copy.start()
-    for s in range(1, trains):
-        load_x[s].start()
-        load_g[s].start()
-    for copy in load_gq + load_xq:
+    for copy in [load_win, load_x[0], load_wout, load_g[0]] + small:
         copy.start()
 
     barrier = pltpu.get_barrier_semaphore()
@@ -96,65 +91,78 @@
 
     repeat(n, greet)
 
+    def first(slot, s, peer, k):
+        return pltpu.make_async_remote_copy(
+            src_ref=held.at[slot, s],
+            dst_ref=held.at[slot, s],
+            send_sem=send_one.at[k, s],
+            recv_sem=recv_one.at[slot, s],
+            device_id={"train": peer},
+            device_id_type=MESH,
+        )
+
     for s in range(trains):
         if s == 0:
             load_win.wait()
         load_x[s].wait()
+        for copy in [load_x[s + 1]] if s + 1 < trains else load_gq:
+            copy.start()
         xp = dot_nt(win_v[...], xt_v[s])
         if s == 0:
             load_wout.wait()
         load_g[s].wait()
+        for copy in [load_g[s + 1]] if s + 1 < trains else load_xq:
+            copy.start()
         gp = dot_nt(wout_v[...], gt_v[s])
         if s == 0:
             for copy in small:
                 copy.wait()
-        length = jnp.full((1, slots), lt_s[s], jnp.int32)
-        scale = jnp.where(lanes((1, slots)) < length, 1.0 / length.astype(F32), 0.0)
-        both = fine(dot_nt, halves(gp * scale), halves(jnp.concatenate([xp, xp], axis=0)))
+        step = lanes((rank, slots))
+        length = jnp.full((rank, slots), lt_s[s], jnp.int32)
+        gp = jnp.where(step < length, gp / length.astype(F32), 0.0)
+        both = fine(dot_nt, halves(gp), halves(jnp.concatenate([xp, xp], axis=0)))
         packed = jnp.where(lanes((rank // 2, 2 * rank)) < rank, both[: rank // 2], both[rank // 2 :])
         held[me, s] = packed.astype(BF16)
-
-    pl.semaphore_wait(barrier, 2 * n - 1)
-
-    def first(slot, peer, k):
-        return pltpu.make_async_remote_copy(
-            src_ref=held.at[slot],
-            dst_ref=held.at[slot],
-            send_sem=send_one.at[k],
-            recv_sem=recv_one.at[slot],
-            device_id={"train": peer},
-            device_id_type=MESH,
-        )
-
-    def send_first(k):
-        first(me, lax.rem(me + 1 + k, n), k).start()
-
-    repeat(n - 1, send_first)
-
-    token = lanes((1, tokens))
+        if s == 0:
+            pl.semaphore_wait(barrier, 2 * n - 1)
+
+        def send_first(k):
+            first(me, s, lax.rem(me + 1 + k, n), k).start()
+
+        repeat(n - 1, send_first)
+
+    step = lanes((1, tokens))
     length = jnp.full((1, tokens), lq_s[0], jnp.int32)
     for j in range(1, queries):
-        length = jnp.where(token // short == j, lq_s[j], length)
-    scale = jnp.where(lax.rem(token, short) < length, 1.0 / length.astype(F32), 0.0)
+        length = jnp.where(step >= j * short, lq_s[j], length)
+    scale = jnp.where(lax.rem(step, short) < length, 1.0 / length.astype(F32), 0.0)
     gp = jnp.zeros((rank, tokens), F32)
     for k, c in enumerate(cut):
         load_gq[k].wait()
         gp += dot_nt(wout_v[:, c], gq_v[:, c])
     gp = fine(dot_nn, halves(fout_v[...]), halves(gp * scale))
-    block = (
-        lanes((1, queries, tokens)) // short == lax.broadcasted_iota(jnp.int32, (1, queries, tokens), 1)
-    ).astype(F32)
-    spread = halves((gp[:, None, :] * block).reshape(rank * queries, tokens))
+    blocks = [
+        jnp.logical_and(step >= j * short, step < (j + 1) * short).astype(F32) for j in range(queries)
+    ]
+    spread = [
+        jnp.concatenate([(term.astype(F32) * block).astype(BF16) for block in blocks], axis=0)
+        for term in halves(gp)
+    ]
     xp = jnp.zeros((rank, tokens), F32)
     for k, c in enumerate(cut):
         load_xq[k].wait()
         xp += dot_nt(win_v[:, c], xq_v[:, c])
-    xp = fine(dot_nn, halves(fin_v[...]), halves(xp))
-    both = fine(dot_nt, spread, halves(jnp.concatenate([xp, xp], axis=0)))
-    rows = rank // 2 * queries
-    query[...] = (
-        jnp.where(lanes((rows, 2 * rank)) < rank, both[:rows], both[rows:]).astype(BF16).astype(F32)
-    )
+    factor = fin_v[...]
+    xp = fine(dot_nn, halves(jnp.concatenate([factor, factor], axis=0)), halves(xp))
+    wide_query[...] = fine(dot_nt, spread, halves(xp))
+    left = lanes((queries, 2 * rank)) < rank
+    for a in range(rank // 2):
+        row = jnp.where(
+            left,
+            wide_query[pl.ds(a, queries, rank), :],
+            wide_query[pl.ds(a + rank // 2, queries, rank), :],
+        )
+        query[a * queries : (a + 1) * queries, :] = row.astype(BF16).astype(F32)
 
     def second(peer, to, where, source, k):
         return pltpu.make_async_remote_copy(
@@ -169,15 +177,12 @@
     def own(k):
         return pltpu.make_async_copy(mine.at[k], landed.at[place, layer], recv_two.at[place, layer])
 
-    def score(k):
-        peer = lax.rem(me + 1 + k, n)
-        if isinstance(k, int):
-            if k < n - 1:
-                first(peer, peer, k).wait_recv()
-        else:
-            @pl.when(k < n - 1)
-            def _():
-                first(peer, peer, k).wait_recv()
+    def score(peer):
+        @pl.when(peer != me)
+        def _():
+            for s in range(trains):
+                first(peer, s, peer, 0).wait_recv()
+
         sums = []
         for s in range(trains):
             wide[...] = held[peer, s].astype(F32)
@@ -185,16 +190,16 @@
             for a in range(rank // 2):
                 total += wide[a : a + 1, :] * query[a * queries : (a + 1) * queries, :]
             sums.append(total + pltpu.roll(total, rank, 1))
-        mine[k] = jnp.where(lanes((queries, 2 * rank)) < rank, sums[0], sums[1])
+        mine[peer] = jnp.where(lanes((queries, 2 * rank)) < rank, sums[0], sums[1])
         local = jnp.logical_and(peer == me, owner == layer)
 
         @pl.when(jnp.logical_not(local))
         def _():
-            second(peer, owner, place, layer, k).start()
+            second(peer, owner, place, layer, peer).start()
 
         @pl.when(local)
         def _():
-            own(k).start()
+            own(peer).start()
 
     repeat(n, score)
 
@@ -209,7 +214,7 @@
 
             @pl.when(local)
             def _():
-                own(n - 1).wait()
+                own(me).wait()
 
     repeat(half, collect)
     total = (landed[:, 0] + landed[:, 1]).reshape(half * queries, 2 * rank)
@@ -222,16 +227,15 @@
     out[...] = result[:trains]
 
     def finish_first(k):
-        first(me, lax.rem(me + 1 + k, n), k).wait_send()
+        for s in range(trains):
+            first(me, s, lax.rem(me + 1 + k, n), k).wait_send()
 
     repeat(n - 1, finish_first)
 
-    def finish_second(k):
-        peer = lax.rem(me + 1 + k, n)
-
+    def finish_second(peer):
         @pl.when(jnp.logical_not(jnp.logical_and(peer == me, owner == layer)))
         def _():
-            second(peer, owner, place, layer, k).wait_send()
+            second(peer, owner, place, layer, peer).wait_send()
 
     repeat(n, finish_second)
 
@@ -245,7 +249,7 @@
     return pl.pallas_call(
         functools.partial(kernel, n),
         out_shape=jax.ShapeDtypeStruct((trains, half * queries), F32),
-        in_specs=[pl.BlockSpec(memory_space=pl.ANY)] * 10,
+        in_specs=[pl.BlockSpec(memory_space=pltpu.HBM)] * 10,
         out_specs=pl.BlockSpec(memory_space=pltpu.VMEM),
         scratch_shapes=[
             pltpu.VMEM((trains, slots, width), BF16),
@@ -260,19 +264,20 @@
             pltpu.SMEM((queries,), jnp.int32),
             pltpu.VMEM((n, trains, rank // 2, 2 * rank), BF16),
             pltpu.VMEM((rank // 2, 2 * rank), F32),
+            pltpu.VMEM((rank * queries, 2 * rank), F32),
             pltpu.VMEM((rank // 2 * queries, 2 * rank), F32),
             pltpu.VMEM((n, queries, 2 * rank), F32),
             pltpu.VMEM((half, 2, queries, 2 * rank), F32),
             pltpu.SemaphoreType.DMA((2 + 2 * trains,)),
             pltpu.SemaphoreType.DMA((2 * SPLITS,)),
             pltpu.SemaphoreType.DMA((4,)),
-            pltpu.SemaphoreType.DMA((n,)),
-            pltpu.SemaphoreType.DMA((n,)),
+            pltpu.SemaphoreType.DMA((n, trains)),
+            pltpu.SemaphoreType.DMA((n, trains)),
             pltpu.SemaphoreType.DMA((n,)),
             pltpu.SemaphoreType.DMA((half, 2)),
         ],
         compiler_params=pltpu.CompilerParams(
-            collective_id=0, has_side_effects=True, vmem_limit_bytes=48 * 1024 * 1024
+            collective_id=0, has_side_effects=True, vmem_limit_bytes=63 * 1024 * 1024
         ),
         cost_estimate=pl.CostEstimate(
             flops=4 * (trains * slots + tokens) * width * rank,

time: 26.8 us -> 19.3 us (0.72)
  the two profiles are of different devices: /device:TPU:0 before, /device:TPU:1 now
where the time goes in v2:
time: 19.3 us; the launch traced here: 19.1 us
  Pallas kernels  17.9 us (93%)
  local copies, waits for them, and re-layouts  1.24 us (6%)
    pallas_call x1, Pallas kernels, on_device(): pl.pallas_call(functools.partial(kernel, n), out_shape=jax.ShapeDtypeStru...  17.9 us
    unnamed x1, local copies, waits for them, and re-layouts  1.24 us

profile of v2, /device:TPU:1, one launch (start us, length us, event | category | flops | bytes accessed | tf_op | source)
XLA Modules:
  0.0 19.1 jit_solution(15191934501194542786)
XLA Ops:
  0.0 17.9 %shard_map.100 = f32[2,32]{1,0:T(2,128)} custom-call(bf16[2,192,4096]{2,1,0:T(8,128)(2,1)} %bitcast.12, bf16[2,192,4096]{2,1,0:T(8,128)(2,1)} %bitcast.13, bf16[256,4096]{1,0:T(8,128)(2,1)} %bitcast.14, bf16[256,4096]{1,0:T(8,128)(2,1)} %bitcast.15, bf16[64,4096]{1,0:T(8,128)(2,1)} %bitcast.16, bf16[64,4096]{1,0:T(8,128)(2,1)} %bitcast.17, ...), custom_call_target="tpu_custom_call" | custom-call | flops 671088640 | bytes 11534336 | tf_op jit(solution)/shard_map/pallas_call | solution.py:249
  17.9 1.2 %copy.12 = f32[2,32]{1,0:T(2,128)} copy(f32[2,32]{1,0:T(2,128)} %shard_map.100) | data formatting | bytes 512

commit v3 on v2

--- a/solution.py
+++ b/solution.py
@@ -69,15 +69,20 @@
         pltpu.make_async_copy(src, dst, small_sem.at[k])
         for k, (src, dst) in enumerate(((lt, lt_s), (lq, lq_s), (fin, fin_v), (fout, fout_v)))
     ]
-    load_win = pltpu.make_async_copy(win, win_v, in_sem.at[0])
-    load_wout = pltpu.make_async_copy(wout, wout_v, in_sem.at[1])
-    load_x = [pltpu.make_async_copy(xt.at[s], xt_v.at[s], in_sem.at[2 + 2 * s]) for s in range(trains)]
-    load_g = [pltpu.make_async_copy(gt.at[s], gt_v.at[s], in_sem.at[3 + 2 * s]) for s in range(trains)]
     cut = [pl.ds(k * part, part) for k in range(SPLITS)]
+
+    def pieces(src, dst, base):
+        return [pltpu.make_async_copy(src.at[:, c], dst.at[:, c], in_sem.at[base, k]) for k, c in enumerate(cut)]
+
+    load_win = pieces(win, win_v, 0)
+    load_wout = pieces(wout, wout_v, 1)
+    load_x = [pieces(xt.at[s], xt_v.at[s], 2 + 2 * s) for s in range(trains)]
+    load_g = [pieces(gt.at[s], gt_v.at[s], 3 + 2 * s) for s in range(trains)]
     load_gq = [pltpu.make_async_copy(gq.at[:, c], gq_v.at[:, c], far_sem.at[k]) for k, c in enumerate(cut)]
     load_xq = [pltpu.make_async_copy(xq.at[:, c], xq_v.at[:, c], far_sem.at[SPLITS + k]) for k, c in enumerate(cut)]
-    for copy in [load_win, load_x[0], load_wout, load_g[0]] + small:
-        copy.start()
+    for pair in list(zip(load_win, load_x[0])) + list(zip(load_wout, load_g[0])) + [small] + load_x[1:] + load_g[1:]:
+        for copy in pair:
+            copy.start()
 
     barrier = pltpu.get_barrier_semaphore()
 
@@ -101,35 +106,47 @@
             device_id_type=MESH,
         )
 
-    for s in range(trains):
-        if s == 0:
-            load_win.wait()
-        load_x[s].wait()
-        for copy in [load_x[s + 1]] if s + 1 < trains else load_gq:
-            copy.start()
-        xp = dot_nt(win_v[...], xt_v[s])
-        if s == 0:
-            load_wout.wait()
-        load_g[s].wait()
-        for copy in [load_g[s + 1]] if s + 1 < trains else load_xq:
-            copy.start()
-        gp = dot_nt(wout_v[...], gt_v[s])
-        if s == 0:
-            for copy in small:
+    def project(weight, rows, copies):
+        total = jnp.zeros((rank, rows.shape[0]), F32)
+        for k, c in enumerate(cut):
+            for copy in copies[k]:
                 copy.wait()
-        step = lanes((rank, slots))
+            total += dot_nt(weight[:, c], rows[:, c])
+        return total
+
+    def gradient(s, xp, gp):
         length = jnp.full((rank, slots), lt_s[s], jnp.int32)
-        gp = jnp.where(step < length, gp / length.astype(F32), 0.0)
+        gp = jnp.where(lanes((rank, slots)) < length, gp / length.astype(F32), 0.0)
         both = fine(dot_nt, halves(gp), halves(jnp.concatenate([xp, xp], axis=0)))
         packed = jnp.where(lanes((rank // 2, 2 * rank)) < rank, both[: rank // 2], both[rank // 2 :])
         held[me, s] = packed.astype(BF16)
-        if s == 0:
-            pl.semaphore_wait(barrier, 2 * n - 1)
-
+
+    def send_gradient(s):
         def send_first(k):
             first(me, s, lax.rem(me + 1 + k, n), k).start()
 
         repeat(n - 1, send_first)
+
+    for s in range(trains):
+        if s == 0:
+            xp = project(win_v, xt_v.at[s], list(zip(load_win, load_x[s])))
+            for copy in load_gq + load_xq:
+                copy.start()
+            gp = project(wout_v, gt_v.at[s], list(zip(load_wout, load_g[s])))
+            for copy in small:
+                copy.wait()
+        else:
+            for copy in load_x[s]:
+                copy.wait()
+            later = dot_nt(win_v[...], xt_v[s])
+            gradient(s - 1, xp, gp)
+            if s == 1:
+                pl.semaphore_wait(barrier, 2 * n - 1)
+            send_gradient(s - 1)
+            xp = later
+            gp = project(wout_v, gt_v.at[s], [[copy] for copy in load_g[s]])
+    gradient(trains - 1, xp, gp)
+    send_gradient(trains - 1)
 
     step = lanes((1, tokens))
     length = jnp.full((1, tokens), lq_s[0], jnp.int32)
@@ -268,7 +285,7 @@
             pltpu.VMEM((rank // 2 * queries, 2 * rank), F32),
             pltpu.VMEM((n, queries, 2 * rank), F32),
             pltpu.VMEM((half, 2, queries, 2 * rank), F32),
-            pltpu.SemaphoreType.DMA((2 + 2 * trains,)),
+            pltpu.SemaphoreType.DMA((2 + 2 * trains, SPLITS)),
             pltpu.SemaphoreType.DMA((2 * SPLITS,)),
             pltpu.SemaphoreType.DMA((4,)),
             pltpu.SemaphoreType.DMA((n, trains)),

time: 19.3 us -> 19.1 us (0.990)
  Pallas kernels: 17.9 us -> 17.7 us
    pallas_call x1, Pallas kernels: 17.9 us -> 17.7 us  [on_device(): pl.pallas_call(functools.partial(kernel, n), out_shape=jax.ShapeDtypeStru...]
where the time goes in v3:
time: 19.1 us; the launch traced here: 18.9 us
  Pallas kernels  17.7 us (93%)
  local copies, waits for them, and re-layouts  1.24 us (6%)
    pallas_call x1, Pallas kernels, on_device(): pl.pallas_call(functools.partial(kernel, n), out_shape=jax.ShapeDtypeStru...  17.7 us
    unnamed x1, local copies, waits for them, and re-layouts  1.24 us

profile of v3, /device:TPU:1, one launch (start us, length us, event | category | flops | bytes accessed | tf_op | source)
XLA Modules:
  0.0 18.9 jit_solution(2733897940846410642)
XLA Ops:
  0.0 17.7 %shard_map.100 = f32[2,32]{1,0:T(2,128)} custom-call(bf16[2,192,4096]{2,1,0:T(8,128)(2,1)} %bitcast.12, bf16[2,192,4096]{2,1,0:T(8,128)(2,1)} %bitcast.13, bf16[256,4096]{1,0:T(8,128)(2,1)} %bitcast.14, bf16[256,4096]{1,0:T(8,128)(2,1)} %bitcast.15, bf16[64,4096]{1,0:T(8,128)(2,1)} %bitcast.16, bf16[64,4096]{1,0:T(8,128)(2,1)} %bitcast.17, ...), custom_call_target="tpu_custom_call" | custom-call | flops 671088640 | bytes 11534336 | tf_op jit(solution)/shard_map/pallas_call | solution.py:266
  17.7 1.2 %copy.12 = f32[2,32]{1,0:T(2,128)} copy(f32[2,32]{1,0:T(2,128)} %shard_map.100) | data formatting | bytes 512
